TPU v7x, 256 devices: a whole 4x4x8 slice. The times are simulated.
256 devices in a mesh: tile: 16 (over y_lo, z), tf: 16 (over x, y_hi, core).
Axes of the slice: x: 4, y: 4 (y_hi: 2, y_lo: 2; y = y_hi * 2 + y_lo), z: 8, core: 2. Of those that a mesh axis runs over, the one named last changes fastest.
Arguments:
- test_field: float32 [16, 3, 16, 256, 1024], P('tf', None, None, 'tile'), may hold values from -6 to 6
- register: float32 [16, 3, 16, 256, 1024], P('tf', None, None, 'tile'), may hold values from -6 to 6
- velocity: bfloat16 [3, 16, 256, 1024], P(None, 'tf', 'tile'), may hold values from -6 to 6
- shear_shift: int32 [2], replicated, may hold values from 0 to 255
Outputs:
- new_field: float32 [16, 3, 16, 256, 1024], P('tf', None, None, 'tile')
- new_register: float32 [16, 3, 16, 256, 1024], P('tf', None, None, 'tile')
Inputs may be any that keep to these rules, and one draw needn't show every extreme that they name: `shear_shift`: the two offsets are independent.
All inputs are finite; a program needn't handle non-finite values.
Results may differ from a plain program's by a relative error of at most 0.0065.
Values may be sent and summed in bfloat16 or wider, within the bound.
A program may use at most 128 MiB of HBM per device.

v0:
```python
import math
import jax
import jax.numpy as jnp
from jax import lax
from jax.sharding import PartitionSpec as P

DIFFUSIVITY = 0.1
TIME_STEP = 0.3
RK_ALPHA = -5.0 / 9.0
RK_BETA = 15.0 / 16.0
SWEEP_SPEED = 0.75
STRETCH_RATE = 0.375


def with_halo(x, sides, width):
    for axis, dim in sides:
        size, length = (lax.axis_size(axis), x.shape[dim])
        up = [(i, (i + 1) % size) for i in range(size)]
        down = [(j, i) for i, j in up]
        last = lax.slice_in_dim(x, length - width, length, axis=dim)
        initial = lax.slice_in_dim(x, 0, width, axis=dim)
        before = lax.ppermute(last, axis, up)
        after = lax.ppermute(initial, axis, down)
        x = jnp.concatenate([before, x, after], axis=dim)
    return x


def first_derivative(shifted):
    return (
        45.0 * (shifted(1) - shifted(-1))
        - 9.0 * (shifted(2) - shifted(-2))
        + (shifted(3) - shifted(-3))
    ) / 60.0


def second_derivative(shifted):
    return (
        -49.0 / 18.0 * shifted(0)
        + 1.5 * (shifted(1) + shifted(-1))
        - 0.15 * (shifted(2) + shifted(-2))
        + (shifted(3) + shifted(-3)) / 90.0
    )


def test_pattern(field_index, planes):
    height = jnp.arange(planes).astype(jnp.float32)
    wavenumber = (field_index // 4 + 1).astype(jnp.float32)
    phase = 2.0 * math.pi * wavenumber[:, None] * height[None, :] / planes
    profile = jnp.where((field_index // 2 % 2 == 0)[:, None], jnp.cos(phase), jnp.sin(phase))
    component = field_index % 2
    selector = (jnp.arange(3)[None, :] == component[:, None]).astype(jnp.float32)
    return (selector[:, :, None] * profile[:, None, :])[:, :, :, None, None]


def cross_emf(velocity, summed):
    vel = velocity.astype(jnp.float32)
    fld = summed.astype(jnp.float32)
    emf_x = vel[1] * fld[:, 2] - vel[2] * fld[:, 1]
    emf_y = vel[2] * fld[:, 0] - vel[0] * fld[:, 2]
    emf_z = vel[0] * fld[:, 1] - vel[1] * fld[:, 0]
    return jnp.stack([emf_x, emf_y, emf_z], 1).astype(jnp.bfloat16)


def tendency(field, view, width):

    def deriv(name, axis, channel):

        def shifted(offset):
            return view(name, axis, offset, channel)

        return first_derivative(shifted)

    def second(axis):

        def shifted(offset):
            return view("field", axis, offset, slice(None))

        return second_derivative(shifted)

    curl_x = deriv("emf", 1, 2) - deriv("emf", 2, 1)
    curl_y = deriv("emf", 2, 0) - deriv("emf", 0, 2)
    curl_z = deriv("emf", 0, 1) - deriv("emf", 1, 0)
    curl = jnp.stack([curl_x, curl_y, curl_z], 1)
    laplace = second(0) + second(1) + second(2)
    field_dy = deriv("field", 1, slice(None))
    xpos = jnp.arange(width).astype(jnp.float32)
    sweep = -SWEEP_SPEED * (2.0 * xpos / (width - 1) - 1.0)
    rate = curl + DIFFUSIVITY * laplace - sweep * field_dy
    return rate.at[:, 1].add(-STRETCH_RATE * field[:, 0])


def make_emf(summed, velocity):
    whole_velocity = lax.all_gather(velocity, "tf", axis=1, tiled=True)
    return cross_emf(whole_velocity, summed)


def body(test_field, register, velocity, shear_shift):
    fields_here = test_field.shape[0]
    rows_here = test_field.shape[3]
    width = test_field.shape[4]
    planes = test_field.shape[2]
    field_index = lax.axis_index("tf") * fields_here + jnp.arange(fields_here)
    pattern = test_pattern(field_index, planes)
    field_rows = with_halo(test_field.astype(jnp.bfloat16), (("tile", 3),), 3).astype(
        test_field.dtype
    )
    summed = (test_field + pattern).astype(jnp.bfloat16)
    emf = make_emf(summed, velocity)
    emf_rows = with_halo(emf, (("tile", 3),), 3)
    lower_source = jnp.concatenate(
        [test_field[..., width - 3 :], emf[..., width - 3 :].astype(jnp.float32)], axis=1
    )
    upper_source = jnp.concatenate([test_field[..., :3], emf[..., :3].astype(jnp.float32)], axis=1)
    strips = jnp.stack([lower_source, upper_source], 1)
    tiles = lax.axis_size("tile")
    whole_strips = lax.all_gather(strips.astype(jnp.bfloat16), "tile", axis=4, tiled=True).astype(
        strips.dtype
    )
    doubled = jnp.concatenate([whole_strips, whole_strips], axis=4)
    total_rows = rows_here * tiles
    sides = []
    for side in range(2):
        start = (lax.axis_index("tile") * rows_here + shear_shift[side]) % total_rows
        sides.append(lax.dynamic_slice_in_dim(doubled[:, side], start, rows_here, 3))
    lower_ghost = sides[0]
    upper_ghost = sides[1]
    padded = {
        "field": jnp.concatenate([lower_ghost[:, :3], test_field, upper_ghost[:, :3]], axis=-1),
        "emf": jnp.concatenate(
            [lower_ghost[:, 3:].astype(jnp.bfloat16), emf, upper_ghost[:, 3:].astype(jnp.bfloat16)],
            axis=-1,
        ),
    }
    rowed = {"field": field_rows, "emf": emf_rows}
    arrays = {"field": test_field, "emf": emf}

    def view(name, axis, offset, channel):
        if axis == 0:
            return padded[name][:, channel][..., 3 + offset : 3 + offset + width].astype(
                jnp.float32
            )
        if axis == 1:
            return lax.slice_in_dim(
                rowed[name][:, channel],
                3 + offset,
                3 + offset + rows_here,
                axis=rowed[name][:, channel].ndim - 2,
            ).astype(jnp.float32)
        return jnp.roll(arrays[name][:, channel], -offset, axis=-3).astype(jnp.float32)

    rate = tendency(test_field, view, width)
    new_register = RK_ALPHA * register + TIME_STEP * rate
    new_field = test_field + RK_BETA * new_register
    return (new_field, new_register)


def solution(mesh):
    return jax.shard_map(
        body,
        mesh=mesh,
        in_specs=(
            P("tf", None, None, "tile", None),
            P("tf", None, None, "tile", None),
            P(None, "tf", "tile", None),
            P(),
        ),
        out_specs=(P("tf", None, None, "tile", None), P("tf", None, None, "tile", None)),
        check_vma=False,
    )
```

profile of v0, /device:TPU:32, one launch (start us, length us, event | category | flops | bytes accessed | tf_op | source)
XLA Modules:
  0.0 211.0 jit_solution(14419312792183972771)
XLA Ops:
  7.2 0.7 all-gather.2.cloned.1.call-update
  7.9 3.8 %copy.196 = bf16[1,3,16,16,1024]{4,2,3,1,0:T(8,128)(2,1)S(1)} copy(f32[1,3,16,16,1024]{4,3,2,1,0:T(8,128)} %param.6) | data formatting | bytes 4718592 | tf_op args[0]
  11.7 1.2 copy-done.8
  12.9 0.9 fusion.42
  13.7 1.9 collective-permute-start.2
  15.7 0.8 fusion.39
  16.5 1.1 fusion.43
  17.8 0.7 fusion.58
  18.5 1.0 fusion.37
  19.5 1.9 fusion.27
  21.4 3.1 %fusion.36 = (f32[1,3,13,16,1024]{4,3,2,1,0:T(8,128)}, f32[1,3,13,16,1024]{4,3,2,1,0:T(8,128)}) fusion(f32[1,3,16,16,1024]{4,3,2,1,0:T(8,128)S(1)} %copy-done), kind=kLoop, calls=%fused_computation.87 | loop fusion | bytes 10223616 | tf_op jit(solution)/shard_map/jit(_roll_static)/slice | solution.py:149
  24.5 3.4 %fusion.38 = (f32[1,3,14,16,1024]{4,3,2,1,0:T(8,128)}, f32[1,3,14,16,1024]{4,3,2,1,0:T(8,128)}) fusion(f32[1,3,16,16,1024]{4,3,2,1,0:T(8,128)S(1)} %copy-done), kind=kLoop, calls=%fused_computation.89 | loop fusion | bytes 11010048 | tf_op jit(solution)/shard_map/jit(_roll_static)/slice | solution.py:149
  27.8 3.5 %fusion.40 = (f32[1,3,15,16,1024]{4,3,2,1,0:T(8,128)}, f32[1,3,15,16,1024]{4,3,2,1,0:T(8,128)}) fusion(f32[1,3,16,16,1024]{4,3,2,1,0:T(8,128)S(1)} %copy-done), kind=kLoop, calls=%fused_computation.91 | loop fusion | bytes 11796480 | tf_op jit(solution)/shard_map/jit(_roll_static)/slice | solution.py:149
  32.7 1.0 copy.179
  33.7 1.0 copy.181
  34.7 1.1 fusion.35
  35.9 0.7 copy-done.9
  36.5 1.3 pad_maximum_fusion.2
  37.9 3.5 %copy_convert_fusion.1 = f32[1,3,16,22,1024]{4,3,2,1,0:T(8,128)} fusion(bf16[1,3,16,22,1024]{4,2,3,1,0:T(8,128)(2,1)S(1)} %pad_maximum_fusion.2), kind=kLoop, calls=%fused_computation.45 | loop fusion | flops 1081344 | bytes 6488064 | tf_op jit(solution)/shard_map/convert_element_type | solution.py:104
  41.3 23.8 %all-gather.2.cloned.1.call-done = bf16[3,16,16,1024]{3,2,0,1:T(8,128)(2,1)} async-done(((bf16[3,1,16,1024]{3,2,0,1:T(8,128)(2,1)}), bf16[3,16,16,1024]{3,2,0,1:T(8,128)(2,1)}) %all-gather.2.cloned.1.call-update) | async-done | bytes 1572880 | tf_op jit(solution)/shard_map/all_gather | solution.py:93
  65.1 1.9 convert_element_type.275
  67.5 0.9 fusion.31
  68.4 0.7 fusion.56
  69.1 0.7 fusion.54
  69.8 0.7 fusion.52
  70.5 0.6 fusion.48
  71.1 0.7 fusion.46
  71.8 1.1 fusion.53
  72.9 1.0 fusion.47
  73.9 1.0 fusion.55
  75.0 1.1 fusion.49
  76.0 1.1 fusion.57
  77.3 1.0 fusion.44
  78.6 1.1 fusion.41
  79.7 1.9 copy.180
  81.6 1.9 copy.182
  83.5 0.9 maximum_bitcast_fusion.1
  84.3 0.7 pad_maximum_fusion.8
  85.0 1.7 copy.183
  86.7 1.8 copy.192
  88.5 0.8 copy.193
  89.8 1.6 collective-permute-start
  91.4 55.9 %all_gather.7 = bf16[1,2,6,16,256,3]{3,1,5,2,0,4:T(2,128)(2,1)} all-gather(bf16[1,2,6,16,16,3]{3,1,5,2,0,4:T(2,128)(2,1)} %copy.183), channel_id=1, replica_groups=mesh['tile'=16,'tf'=16] {'tile'}, dimensions={4}, use_global_device_ids=true | all-gather | bytes 313344 | tf_op jit(solution)/shard_map/all_gather | solution.py:116
  147.3 5.4 %copy.184 = bf16[1,2,6,16,256,3]{4,3,5,2,1,0:T(8,128)(2,1)S(1)} copy(bf16[1,2,6,16,256,3]{3,1,5,2,0,4:T(2,128)(2,1)} %all_gather.7) | data formatting | bytes 589824 | tf_op jit(solution)/shard_map/all_gather | solution.py:116
  153.1 0.7 slice.727
  153.9 0.6 copy-done.21
  154.9 1.1 copy.187
  156.0 4.3 %concatenate.289 = bf16[1,3,16,16,1030]{4,3,2,1,0:T(8,128)(2,1)} concatenate(bf16[1,3,16,16,3]{4,3,2,1,0:T(8,128)(2,1)S(1)} %copy.186, bf16[1,3,16,16,1024]{4,3,2,1,0:T(8,128)(2,1)} %copy-done.7, bf16[1,3,16,16,3]{4,3,2,1,0:T(8,128)(2,1)S(1)} %copy.187), dimensions={4} | concatenate | bytes 3164160 | tf_op jit(solution)/shard_map/concatenate | solution.py:129
  160.4 2.2 %slice_bitcast_fusion.4 = (bf16[1,16,16,1030]{3,2,0,1:T(8,128)(2,1)S(1)}, bf16[1,16,16,1030]{3,2,0,1:T(8,128)(2,1)}) fusion(bf16[1,3,16,16,1030]{4,3,2,1,0:T(8,128)(2,1)} %concatenate.289), kind=kLoop, calls=%fused_computation.72 | loop fusion | bytes 2109440 | tf_op jit(solution)/shard_map/squeeze | solution.py:139
  162.5 3.7 %subtract_bitcast_fusion.1 = f32[1,1,16,16,1024]{4,3,2,1,0:T(8,128)} fusion(bf16[1,16,16,1030]{3,2,0,1:T(8,128)(2,1)S(1)} %get-tuple-element.35, bf16[1,1,16,1024]{3,2,0,1:T(8,128)(2,1)} %get-tuple-element.68, bf16[1,15,16,1024]{3,2,0,1:T(8,128)(2,1)} %get-tuple-element.70, bf16[1,15,16,1024]{3,2,0,1:T(8,128)(2,1)} %get-tuple-element.69, ...), kind=kLoop, calls=%fused_computation.62 | loop fusion | flops 9175040 | bytes 7340032 | tf_op jit(solution)/shard_map/stack | solution.py:83
  166.2 1.4 fusion.50
  167.6 0.6 slice.577
  168.2 0.6 slice.580
  168.9 1.2 copy.189
  170.1 2.0 copy.188
  172.1 1.4 fusion.51
  173.6 1.3 copy.177
  174.9 1.2 copy.176
  176.1 0.8 maximum_bitcast_fusion
  177.1 2.5 %subtract_bitcast_fusion = f32[1,1,16,16,1024]{4,3,2,1,0:T(8,128)} fusion(bf16[1,16,22,1024]{3,2,0,1:T(8,128)(2,1)S(1)} %get-tuple-element.34, bf16[1,16,16,1030]{3,2,0,1:T(8,128)(2,1)S(1)} %copy-done.5), kind=kLoop, calls=%fused_computation.61 | loop fusion | flops 7602176 | bytes 7340032 | tf_op jit(solution)/shard_map/stack | solution.py:83
  179.7 2.1 subtract_bitcast_fusion.2
  181.8 13.7 %fusion.9 = f32[1,3,16,16,1024]{4,3,2,1,0:T(8,128)} fusion(f32[1,3,16,16,1024]{4,3,2,1,0:T(8,128)S(1)} %copy-done, f32[1,3,16,16,3]{4,3,2,1,0:T(8,128)S(1)} %copy.189, f32[1,3,16,16,3]{4,3,2,1,0:T(8,128)} %copy.188, f32[1,3,16,22,1024]{4,3,2,1,0:T(8,128)S(1)} %bitcast.80, f32[1,1,16,16,1024]{4,3,2,1,0:T(8,128)} %subtract_bitcast_fusion, ...), kind=kLoop, calls=%fused_computation.17 | loop fusion | flops 44040192 | bytes 50354176 | tf_op jit(solution)/shard_map/sub | solution.py:88
  195.5 2.6 %fusion.28 = f32[1,3,16,16,1024]{4,3,2,1,0:T(8,128)} fusion(f32[1,3,16,16,1024]{4,3,2,1,0:T(8,128)} %fusion.9, f32[1,3,16,16,1024]{4,3,2,1,0:T(8,128)S(1)} %copy-done), kind=kLoop, calls=%fused_computation.50 | loop fusion | flops 524288 | bytes 3145728 | tf_op jit(solution)/shard_map/scatter-add | solution.py:89
  198.0 6.1 %multiply_add_fusion = (f32[1,3,16,16,1024]{4,3,2,1,0:T(8,128)}, f32[1,3,16,16,1024]{4,3,2,1,0:T(8,128)}) fusion(f32[1,3,16,16,1024]{4,3,2,1,0:T(8,128)S(1)} %copy-done, f32[1,3,16,16,1024]{4,3,2,1,0:T(8,128)} %fusion.28, f32[1,3,16,16,1024]{4,3,2,1,0:T(8,128)S(1)} %copy-done.13), kind=kLoop, calls=%fused_computation.42 | loop fusion | flops 3932160 | bytes 15728640 | tf_op jit(solution)/shard_map/add | solution.py:153
  (80 shorter events, 2.6 us)
Async XLA Ops:
  7.2 8.6 %copy-start = (f32[1,3,16,16,1024]{4,3,2,1,0:T(8,128)S(1)}, f32[1,3,16,16,1024]{4,3,2,1,0:T(8,128)}, u32[]{:S(2)}) copy-start(f32[1,3,16,16,1024]{4,3,2,1,0:T(8,128)} %param.6) | copy-start | bytes 9437188
  7.2 58.0 %all-gather.2.cloned.1.call-start = ((), (), s32[]{:S(2)}) async-start(), calls=%async_computation | async-start | bytes 1671168 | tf_op jit(solution)/shard_map/all_gather | solution.py:93
  7.9 9.9 %copy-start.29 = (s32[2]{0:T(128)S(1)}, s32[2]{0:T(128)}, u32[]{:S(2)}) copy-start(s32[2]{0:T(128)} %param.9) | copy-start | bytes 28
  11.7 1.2 copy-start.8
  13.7 22.1 %collective-permute-start.2 = (bf16[1,3,16,3,1024]{4,2,3,1,0:T(8,128)(2,1)}, bf16[1,3,16,3,1024]{4,2,3,1,0:T(8,128)(2,1)}, u32[]{:S(2)}, u32[]{:S(2)}) collective-permute-start(bf16[1,3,16,3,1024]{4,2,3,1,0:T(8,128)(2,1)} %get-tuple-element.39), channel_id=1, source_target_pairs={{0,16},{16,32},{32,48},{48,64},{64,80},{80,96},{96,112},{112,128},... | collective-permute-start | bytes 884744 | tf_op jit(solution)/shard_map/ppermute | solution.py:22
  15.6 20.2 %collective-permute-start.3 = (bf16[1,3,16,3,1024]{4,2,3,1,0:T(8,128)(2,1)}, bf16[1,3,16,3,1024]{4,2,3,1,0:T(8,128)(2,1)}, u32[]{:S(2)}, u32[]{:S(2)}) collective-permute-start(bf16[1,3,16,3,1024]{4,2,3,1,0:T(8,128)(2,1)} %get-tuple-element.40), channel_id=1, source_target_pairs={{16,0},{32,16},{48,32},{64,48},{80,64},{96,80},{112,96},{128,112},... | collective-permute-start | bytes 884744 | tf_op jit(solution)/shard_map/ppermute | solution.py:23
  34.7 1.8 copy-start.9
  65.1 2.4 %copy-start.6 = (f32[1,3,16,16,1024]{4,3,2,1,0:T(8,128)S(1)}, f32[1,3,16,16,1024]{4,3,2,1,0:T(8,128)}, u32[]{:S(2)}) copy-start(f32[1,3,16,16,1024]{4,3,2,1,0:T(8,128)} %fusion.27) | copy-start | bytes 9437188
  68.4 8.7 %copy-start.1 = (bf16[1,16,16,1024]{3,2,0,1:T(8,128)(2,1)}, bf16[1,16,16,1024]{3,2,0,1:T(8,128)(2,1)S(1)}, u32[]{:S(2)}) copy-start(bf16[1,16,16,1024]{3,2,0,1:T(8,128)(2,1)S(1)} %get-tuple-element.18) | copy-start | bytes 1572868
  68.4 8.7 %copy-start.3 = (bf16[1,16,16,1024]{3,2,0,1:T(8,128)(2,1)}, bf16[1,16,16,1024]{3,2,0,1:T(8,128)(2,1)S(1)}, u32[]{:S(2)}) copy-start(bf16[1,16,16,1024]{3,2,0,1:T(8,128)(2,1)S(1)} %get-tuple-element.19) | copy-start | bytes 1572868
  68.4 8.7 %copy-start.10 = (bf16[1,1,16,16,1024]{4,3,2,1,0:T(8,128)(2,1)}, bf16[1,1,16,16,1024]{4,3,2,1,0:T(8,128)(2,1)S(1)}, u32[]{:S(2)}) copy-start(bf16[1,1,16,16,1024]{4,3,2,1,0:T(8,128)(2,1)S(1)} %get-tuple-element.20) | copy-start | bytes 1572868
  77.3 1.3 copy-start.7
  89.4 84.2 %collective-permute-start.1 = (bf16[1,3,16,3,1024]{4,2,3,1,0:T(8,128)(2,1)}, bf16[1,3,16,3,1024]{4,2,3,1,0:T(8,128)(2,1)}, u32[]{:S(2)}, u32[]{:S(2)}) collective-permute-start(bf16[1,3,16,3,1024]{4,2,3,1,0:T(8,128)(2,1)} %copy.193), channel_id=1, source_target_pairs={{16,0},{32,16},{48,32},{64,48},{80,64},{96,80},{112,96},{128,112},... | collective-permute-start | bytes 884744 | tf_op jit(solution)/shard_map/ppermute | solution.py:23
  89.8 85.0 %collective-permute-start = (bf16[1,3,16,3,1024]{4,2,3,1,0:T(8,128)(2,1)}, bf16[1,3,16,3,1024]{4,2,3,1,0:T(8,128)(2,1)}, u32[]{:S(2)}, u32[]{:S(2)}) collective-permute-start(bf16[1,3,16,3,1024]{4,2,3,1,0:T(8,128)(2,1)} %copy.192), channel_id=1, source_target_pairs={{0,16},{16,32},{32,48},{48,64},{64,80},{80,96},{96,112},{112,128},... | collective-permute-start | bytes 884744 | tf_op jit(solution)/shard_map/ppermute | solution.py:22
  153.1 0.8 copy-start.19
  153.8 0.7 copy-start.21
  162.5 5.1 %copy-start.20 = (f32[1,6,16,16,3]{3,2,4,1,0:T(8,128)S(1)}, f32[1,6,16,16,3]{3,2,4,1,0:T(8,128)}, u32[]{:S(2)}) copy-start(f32[1,6,16,16,3]{3,2,4,1,0:T(8,128)} %copy-done.19) | copy-start | bytes 55300
  162.5 5.7 %copy-start.22 = (f32[1,6,16,16,3]{3,2,4,1,0:T(8,128)S(1)}, f32[1,6,16,16,3]{3,2,4,1,0:T(8,128)}, u32[]{:S(2)}) copy-start(f32[1,6,16,16,3]{3,2,4,1,0:T(8,128)} %copy-done.21) | copy-start | bytes 55300
  172.1 3.9 %copy-start.2 = (bf16[1,16,16,1024]{3,2,0,1:T(8,128)(2,1)S(1)}, bf16[1,16,16,1024]{3,2,0,1:T(8,128)(2,1)}, u32[]{:S(2)}) copy-start(bf16[1,16,16,1024]{3,2,0,1:T(8,128)(2,1)} %copy-done.1) | copy-start | bytes 1572868
  172.1 3.9 %copy-start.4 = (bf16[1,16,16,1024]{3,2,0,1:T(8,128)(2,1)S(1)}, bf16[1,16,16,1024]{3,2,0,1:T(8,128)(2,1)}, u32[]{:S(2)}) copy-start(bf16[1,16,16,1024]{3,2,0,1:T(8,128)(2,1)} %copy-done.3) | copy-start | bytes 1572868
  172.1 4.0 %copy-start.11 = (bf16[1,1,16,16,1024]{4,3,2,1,0:T(8,128)(2,1)S(1)}, bf16[1,1,16,16,1024]{4,3,2,1,0:T(8,128)(2,1)}, u32[]{:S(2)}) copy-start(bf16[1,1,16,16,1024]{4,3,2,1,0:T(8,128)(2,1)} %copy-done.10) | copy-start | bytes 1572868
  173.5 3.4 %copy-start.5 = (bf16[1,16,16,1030]{3,2,0,1:T(8,128)(2,1)S(1)}, bf16[1,16,16,1030]{3,2,0,1:T(8,128)(2,1)}, u32[]{:S(2)}) copy-start(bf16[1,16,16,1030]{3,2,0,1:T(8,128)(2,1)} %get-tuple-element.36) | copy-start | bytes 1582084
  176.1 5.6 %slice-start = ((s8[4718592]{0:T(1024)(128)(4,1)}), s8[4194304]{0:T(1024)(128)(4,1)S(1)}, s32[]{:S(2)}) async-start(s8[4718592]{0:T(1024)(128)(4,1)} %bitcast.79), calls=%async_computation.1 | async-start | bytes 8388608
  176.9 2.6 %copy-start.15 = (bf16[1,14,16,1024]{3,2,0,1:T(8,128)(2,1)S(1)}, bf16[1,14,16,1024]{3,2,0,1:T(8,128)(2,1)}, u32[]{:S(2)}) copy-start(bf16[1,14,16,1024]{3,2,0,1:T(8,128)(2,1)} %get-tuple-element.53) | copy-start | bytes 1376260
  177.0 2.6 %copy-start.16 = (bf16[1,14,16,1024]{3,2,0,1:T(8,128)(2,1)S(1)}, bf16[1,14,16,1024]{3,2,0,1:T(8,128)(2,1)}, u32[]{:S(2)}) copy-start(bf16[1,14,16,1024]{3,2,0,1:T(8,128)(2,1)} %get-tuple-element.54) | copy-start | bytes 1376260
  177.0 2.6 %copy-start.17 = (bf16[1,13,16,1024]{3,2,0,1:T(8,128)(2,1)S(1)}, bf16[1,13,16,1024]{3,2,0,1:T(8,128)(2,1)}, u32[]{:S(2)}) copy-start(bf16[1,13,16,1024]{3,2,0,1:T(8,128)(2,1)} %get-tuple-element.49) | copy-start | bytes 1277956
  177.0 2.6 %copy-start.18 = (bf16[1,13,16,1024]{3,2,0,1:T(8,128)(2,1)S(1)}, bf16[1,13,16,1024]{3,2,0,1:T(8,128)(2,1)}, u32[]{:S(2)}) copy-start(bf16[1,13,16,1024]{3,2,0,1:T(8,128)(2,1)} %get-tuple-element.50) | copy-start | bytes 1277956
  177.0 2.6 %copy-start.23 = (bf16[1,3,16,1024]{3,2,0,1:T(8,128)(2,1)S(1)}, bf16[1,3,16,1024]{3,2,0,1:T(8,128)(2,1)}, u32[]{:S(2)}) copy-start(bf16[1,3,16,1024]{3,2,0,1:T(8,128)(2,1)} %get-tuple-element.47) | copy-start | bytes 294916
  177.0 2.6 %copy-start.24 = (bf16[1,3,16,1024]{3,2,0,1:T(8,128)(2,1)S(1)}, bf16[1,3,16,1024]{3,2,0,1:T(8,128)(2,1)}, u32[]{:S(2)}) copy-start(bf16[1,3,16,1024]{3,2,0,1:T(8,128)(2,1)} %get-tuple-element.48) | copy-start | bytes 294916
  177.0 2.6 %copy-start.25 = (bf16[1,2,16,1024]{3,2,0,1:T(8,128)(2,1)S(1)}, bf16[1,2,16,1024]{3,2,0,1:T(8,128)(2,1)}, u32[]{:S(2)}) copy-start(bf16[1,2,16,1024]{3,2,0,1:T(8,128)(2,1)} %get-tuple-element.51) | copy-start | bytes 196612
  177.0 2.6 %copy-start.26 = (bf16[1,2,16,1024]{3,2,0,1:T(8,128)(2,1)S(1)}, bf16[1,2,16,1024]{3,2,0,1:T(8,128)(2,1)}, u32[]{:S(2)}) copy-start(bf16[1,2,16,1024]{3,2,0,1:T(8,128)(2,1)} %get-tuple-element.52) | copy-start | bytes 196612
  177.0 2.6 %copy-start.27 = (bf16[1,1,16,1024]{3,2,0,1:T(8,128)(2,1)S(1)}, bf16[1,1,16,1024]{3,2,0,1:T(8,128)(2,1)}, u32[]{:S(2)}) copy-start(bf16[1,1,16,1024]{3,2,0,1:T(8,128)(2,1)} %get-tuple-element.55) | copy-start | bytes 98308
  177.0 2.6 %copy-start.28 = (bf16[1,1,16,1024]{3,2,0,1:T(8,128)(2,1)S(1)}, bf16[1,1,16,1024]{3,2,0,1:T(8,128)(2,1)}, u32[]{:S(2)}) copy-start(bf16[1,1,16,1024]{3,2,0,1:T(8,128)(2,1)} %get-tuple-element.56) | copy-start | bytes 98308
  177.0 4.7 %slice-start.1 = ((s8[4718592]{0:T(1024)(128)(4,1)}), s8[524288]{0:T(1024)(128)(4,1)S(1)}, s32[]{:S(2)}) async-start(s8[4718592]{0:T(1024)(128)(4,1)} %bitcast.79), calls=%async_computation.2 | async-start | bytes 1048576
  179.6 2.1 %copy-start.12 = (f32[1,1,16,16,1024]{4,3,2,1,0:T(8,128)S(1)}, f32[1,1,16,16,1024]{4,3,2,1,0:T(8,128)}, u32[]{:S(2)}) copy-start(f32[1,1,16,16,1024]{4,3,2,1,0:T(8,128)} %subtract_bitcast_fusion.1) | copy-start | bytes 3145732
  179.6 2.1 %copy-start.14 = (f32[1,3,3,16,1024]{4,3,2,1,0:T(8,128)S(1)}, f32[1,3,3,16,1024]{4,3,2,1,0:T(8,128)}, u32[]{:S(2)}) copy-start(f32[1,3,3,16,1024]{4,3,2,1,0:T(8,128)} %get-tuple-element.21) | copy-start | bytes 1769476
  195.4 2.6 %copy-start.13 = (f32[1,3,16,16,1024]{4,3,2,1,0:T(8,128)S(1)}, f32[1,3,16,16,1024]{4,3,2,1,0:T(8,128)}, u32[]{:S(2)}) copy-start(f32[1,3,16,16,1024]{4,3,2,1,0:T(8,128)} %param.7) | copy-start | bytes 9437188
Sparse Core Ops, SparseCore 0:
  10.7 54.3 all-gather.1
where the time goes:
time: 212 us; the launch traced here: 211 us
  local copies, waits for them, and re-layouts  67.8 us (32%)
  blocking collectives  55.9 us (26%)
  other arithmetic  42.9 us (20%)
  waiting for transfers between devices  24.5 us (12%)
  between operations  15.8 us (7%)
  starting transfers between devices  4.09 us (2%)
    all_gather x1, blocking collectives, body(): lax.all_gather(strips.astype(jnp.bfloat16), 'tile', axis=4, tiled=True)  55.9 us
    slice x18, local copies, waits for them, and re-layouts, view(): jnp.roll(arrays[name][:, channel], -offset, axis=-3).astype(jnp.float32)  24.3 us
    all_gather x1, waiting for transfers between devices, make_emf(): whole_velocity = lax.all_gather(velocity, 'tf', axis=1, tiled=True)  23.8 us
    sub x1, other arithmetic, tendency(): rate = curl + DIFFUSIVITY * laplace - sweep * field_dy  13.7 us
    unnamed x67, local copies, waits for them, and re-layouts  9.79 us
    another operation x3, other arithmetic, tendency(): curl = jnp.stack([curl_x, curl_y, curl_z], 1)  8.25 us
    add x1, other arithmetic, body(): new_field = test_field + RK_BETA * new_register  6.1 us
    all_gather x1, local copies, waits for them, and re-layouts, body(): lax.all_gather(strips.astype(jnp.bfloat16), 'tile', axis=4, tiled=True)  5.4 us
  transfers between devices with their start and end apart: 5, of which 1 were waited for; matrix products, arithmetic and copies ran while one was open for 26% of the time, Pallas kernels for 0%

commit v1 on v0

--- a/solution.py
+++ b/solution.py
@@ -90,7 +90,9 @@
 
 
 def make_emf(summed, velocity):
-    whole_velocity = lax.all_gather(velocity, "tf", axis=1, tiled=True)
+    whole_velocity = jnp.concatenate(
+        lax.all_to_all(jnp.stack([velocity] * lax.axis_size("tf")), "tf", 0, 0), axis=1
+    )
     return cross_emf(whole_velocity, summed)
 
 

time: 212 us -> 173 us (0.82)
  the two profiles are of different devices: /device:TPU:32 before, /device:TPU:8 now
where the time goes in v1:
time: 173 us
  blocking collectives  55.1 us (32%)
  local copies, waits for them, and re-layouts  52.1 us (30%)
  other arithmetic  42.6 us (25%)
  starting transfers between devices  18.3 us (11%)
  between operations  2.49 us (1%)
  waiting for transfers between devices  1.88 us (1%)
    all_gather x1, blocking collectives, body(): lax.all_gather(strips.astype(jnp.bfloat16), 'tile', axis=4, tiled=True)  55.1 us
    slice x18, local copies, waits for them, and re-layouts, view(): jnp.roll(arrays[name][:, channel], -offset, axis=-3).astype(jnp.float32)  21.6 us
    sub x1, other arithmetic, tendency(): rate = curl + DIFFUSIVITY * laplace - sweep * field_dy  13.7 us
    ppermute x2, starting transfers between devices, with_halo(): after = lax.ppermute(initial, axis, down)  10.1 us
    another operation x3, other arithmetic, tendency(): curl = jnp.stack([curl_x, curl_y, curl_z], 1)  7.54 us
    all_to_all x1, starting transfers between devices, make_emf(): lax.all_to_all(jnp.stack([velocity] * lax.axis_size('tf')), 'tf', 0, 0)  6.18 us
    add x1, other arithmetic, body(): new_field = test_field + RK_BETA * new_register  6.1 us
    all_gather x1, local copies, waits for them, and re-layouts, body(): lax.all_gather(strips.astype(jnp.bfloat16), 'tile', axis=4, tiled=True)  5.4 us
  transfers between devices with their start and end apart: 5, of which 1 were waited for; matrix products, arithmetic and copies ran while one was open for 27% of the time, Pallas kernels for 0%

profile of v1, /device:TPU:8, one launch (start us, length us, event | category | flops | bytes accessed | tf_op | source)
XLA Modules:
  0.0 172.6 jit_solution(8307294914133583723)
XLA Ops:
  0.6 2.4 %stack.24 = bf16[16,3,1,16,1024]{4,3,2,1,0:T(8,128)(2,1)} broadcast(bf16[3,16,1024]{2,1,0:T(8,128)(2,1)} %bitcast.91), dimensions={1,3,4} | broadcast | bytes 1671168 | tf_op jit(solution)/shard_map/stack | solution.py:94
  3.1 6.2 %all-to-all-start = ((bf16[16,3,1,16,1024]{4,3,2,1,0:T(8,128)(2,1)}), bf16[16,3,1,16,1024]{4,3,2,1,0:T(8,128)(2,1)}, u32[]{:S(2)}, u32[]{:S(2)}) async-start(bf16[16,3,1,16,1024]{4,3,2,1,0:T(8,128)(2,1)} %stack.24), calls=%async_computation | async-start | bytes 3145728 | tf_op jit(solution)/shard_map/all_to_all | solution.py:94
  9.4 2.2 %fusion.37 = (bf16[1,3,16,16,1024]{4,3,2,1,0:T(8,128)(2,1)S(1)}, f32[1,3,16,16,1024]{4,3,2,1,0:T(8,128)}) fusion(f32[1,3,16,16,1024]{4,3,2,1,0:T(8,128)S(1)} %copy-done, f32[3,16]{1,0:T(4,128)S(1)} %broadcast_multiply_fusion), kind=kLoop, calls=%fused_computation.89 | loop fusion | flops 3145728 | bytes 7864512 | tf_op jit(solution)/shard_map/convert.13
  11.6 1.4 fusion.39
  13.0 1.9 %collective-permute-start.2 = (bf16[1,3,16,3,1024]{4,3,2,1,0:T(4,128)(2,1)}, bf16[1,3,16,3,1024]{4,3,2,1,0:T(4,128)(2,1)}, u32[]{:S(2)}, u32[]{:S(2)}) collective-permute-start(bf16[1,3,16,3,1024]{4,3,2,1,0:T(4,128)(2,1)} %get-tuple-element.39), channel_id=1, source_target_pairs={{0,16},{16,32},{32,48},{48,64},{64,80},{80,96},{96,112},{112,128},... | collective-permute-start | bytes 884744 | tf_op jit(solution)/shard_map/ppermute | solution.py:22
  14.9 4.7 %collective-permute-start.3 = (bf16[1,3,16,3,1024]{4,3,2,1,0:T(4,128)(2,1)}, bf16[1,3,16,3,1024]{4,3,2,1,0:T(4,128)(2,1)}, u32[]{:S(2)}, u32[]{:S(2)}) collective-permute-start(bf16[1,3,16,3,1024]{4,3,2,1,0:T(4,128)(2,1)} %get-tuple-element.40), channel_id=1, source_target_pairs={{16,0},{32,16},{48,32},{64,48},{80,64},{96,80},{112,96},{128,112},... | collective-permute-start | bytes 884744 | tf_op jit(solution)/shard_map/ppermute | solution.py:23
  19.7 0.8 fusion.35
  20.4 1.0 fusion.33
  21.4 0.1 fusion.40
  21.6 3.3 %fusion.34 = (f32[1,3,14,16,1024]{4,3,2,1,0:T(8,128)}, f32[1,3,14,16,1024]{4,3,2,1,0:T(8,128)}) fusion(f32[1,3,16,16,1024]{4,3,2,1,0:T(8,128)S(1)} %copy-done), kind=kLoop, calls=%fused_computation.86 | loop fusion | bytes 11010048 | tf_op jit(solution)/shard_map/jit(_roll_static)/slice | solution.py:151
  24.9 0.6 fusion.55
  25.5 3.0 %fusion.32 = (f32[1,3,13,16,1024]{4,3,2,1,0:T(8,128)}, f32[1,3,13,16,1024]{4,3,2,1,0:T(8,128)}) fusion(f32[1,3,16,16,1024]{4,3,2,1,0:T(8,128)S(1)} %copy-done), kind=kLoop, calls=%fused_computation.84 | loop fusion | bytes 10223616 | tf_op jit(solution)/shard_map/jit(_roll_static)/slice | solution.py:151
  28.6 3.5 %fusion.36 = (f32[1,3,15,16,1024]{4,3,2,1,0:T(8,128)}, f32[1,3,15,16,1024]{4,3,2,1,0:T(8,128)}) fusion(f32[1,3,16,16,1024]{4,3,2,1,0:T(8,128)S(1)} %copy-done), kind=kLoop, calls=%fused_computation.88 | loop fusion | bytes 11796480 | tf_op jit(solution)/shard_map/jit(_roll_static)/slice | solution.py:151
  33.4 1.0 copy.16
  34.5 1.0 copy.18
  35.5 1.2 fusion.31
  36.7 1.9 %collective-permute-done.2 = bf16[1,3,16,3,1024]{4,3,2,1,0:T(4,128)(2,1)} collective-permute-done((bf16[1,3,16,3,1024]{4,3,2,1,0:T(4,128)(2,1)}, bf16[1,3,16,3,1024]{4,3,2,1,0:T(4,128)(2,1)}, u32[]{:S(2)}, u32[]{:S(2)}) %collective-permute-start.2) | collective-permute-done | bytes 294944 | tf_op jit(solution)/shard_map/ppermute | solution.py:22
  38.6 4.3 %maximum_convert_fusion = f32[1,3,16,22,1024]{4,3,2,1,0:T(8,128)} fusion(bf16[1,3,16,3,1024]{4,3,2,1,0:T(4,128)(2,1)} %collective-permute-done.3, bf16[1,3,16,16,1024]{4,3,2,1,0:T(8,128)(2,1)S(1)} %copy-done.7, bf16[1,3,16,3,1024]{4,3,2,1,0:T(4,128)(2,1)} %collective-permute-done.2), kind=kLoop, calls=%fused_computation.45 | loop fusion | flops 6488064 | bytes 6488064 | tf_op jit(solution)/shard_map/convert_element_type | solution.py:106
  42.9 1.9 %convert_bitcast_fusion = f32[3,16,1,16,1024]{4,3,2,0,1:T(8,128)S(1)} fusion(bf16[16,3,1,16,1024]{4,3,2,1,0:T(8,128)(2,1)} %all-to-all-done), kind=kLoop, calls=%fused_computation.41 | loop fusion | flops 786432 | bytes 4718592 | tf_op jit(solution)/shard_map/convert_element_type | solution.py:56
  44.9 0.4 copy-done.5
  45.3 0.9 subtract_convert_fusion.2
  46.2 0.7 fusion.53
  46.9 0.6 fusion.51
  47.5 0.7 fusion.49
  48.2 0.7 fusion.45
  48.9 0.7 fusion.43
  49.6 1.1 fusion.50
  50.6 1.0 fusion.44
  51.7 1.0 fusion.52
  52.7 1.1 fusion.46
  53.8 1.1 fusion.54
  54.8 0.2 pad_maximum_fusion.2
  55.0 0.1 fusion.41
  55.2 1.0 copy-done.8
  56.2 1.2 fusion.38
  57.5 1.0 copy.17
  58.5 0.4 copy.19
  58.9 0.8 maximum_bitcast_fusion.1
  59.8 0.1 copy.20
  59.9 0.1 collective-permute-start
  60.0 5.4 %collective-permute-start.1 = (bf16[1,3,16,3,1024]{4,3,2,1,0:T(4,128)(2,1)}, bf16[1,3,16,3,1024]{4,3,2,1,0:T(4,128)(2,1)}, u32[]{:S(2)}, u32[]{:S(2)}) collective-permute-start(bf16[1,3,16,3,1024]{4,3,2,1,0:T(4,128)(2,1)} %get-tuple-element.38), channel_id=1, source_target_pairs={{16,0},{32,16},{48,32},{64,48},{80,64},{96,80},{112,96},{128,112},... | collective-permute-start | bytes 884744 | tf_op jit(solution)/shard_map/ppermute | solution.py:23
  65.4 55.1 %all_gather.3 = bf16[1,2,6,16,256,3]{3,1,5,2,0,4:T(2,128)(2,1)} all-gather(bf16[1,2,6,16,16,3]{3,1,5,2,0,4:T(2,128)(2,1)S(1)} %copy.20), channel_id=1, replica_groups=mesh['tile'=16,'tf'=16] {'tile'}, dimensions={4}, use_global_device_ids=true | all-gather | bytes 313344 | tf_op jit(solution)/shard_map/all_gather | solution.py:118
  120.6 5.4 %copy.21 = bf16[1,2,6,16,256,3]{4,3,5,2,1,0:T(8,128)(2,1)S(1)} copy(bf16[1,2,6,16,256,3]{3,1,5,2,0,4:T(2,128)(2,1)} %all_gather.3) | data formatting | bytes 589824 | tf_op jit(solution)/shard_map/all_gather | solution.py:118
  126.0 0.1 maximum_convert_fusion.1
  126.1 1.0 fusion.42
  127.0 0.1 constant_dynamic-slice_fusion.1
  127.1 1.5 copy.23
  128.7 1.0 slice.749
  129.7 1.1 constant_dynamic-slice_fusion
  130.8 1.5 copy.24
  132.3 1.0 slice.748
  133.3 4.3 %concatenate.289 = bf16[1,3,16,16,1030]{4,3,2,1,0:T(8,128)(2,1)} concatenate(bf16[1,3,16,16,3]{4,3,2,1,0:T(8,128)(2,1)S(1)} %slice.749, bf16[1,3,16,16,1024]{4,3,2,1,0:T(8,128)(2,1)} %copy-done.8, bf16[1,3,16,16,3]{4,3,2,1,0:T(8,128)(2,1)S(1)} %slice.748), dimensions={4} | concatenate | bytes 3164160 | tf_op jit(solution)/shard_map/concatenate | solution.py:131
  137.7 1.3 slice_bitcast_fusion.7
  139.0 3.0 %subtract_bitcast_fusion.1 = f32[1,1,16,16,1024]{4,3,2,1,0:T(8,128)S(1)} fusion(bf16[1,16,16,1030]{3,2,1,0:T(8,128)(2,1)S(1)} %get-tuple-element.35, bf16[1,1,16,1024]{3,2,1,0:T(8,128)(2,1)} %get-tuple-element.68, bf16[1,15,16,1024]{3,2,1,0:T(8,128)(2,1)} %get-tuple-element.70, bf16[1,15,16,1024]{3,2,1,0:T(8,128)(2,1)} %get-tuple-element.69, ...), kind=kLoop, calls=%fused_computation.57 | loop fusion | flops 9175040 | bytes 7340032 | tf_op jit(solution)/shard_map/stack | solution.py:83
  142.1 0.8 slice.589
  142.9 0.1 fusion.48
  143.0 0.1 copy-done.2
  143.1 0.3 copy-done.10
  143.4 2.1 %maximum_bitcast_fusion = (bf16[1,16,22,1024]{3,2,1,0:T(8,128)(2,1)S(1)}, bf16[1,16,22,1024]{3,2,1,0:T(8,128)(2,1)S(1)}) fusion(bf16[1,3,16,3,1024]{4,3,2,1,0:T(4,128)(2,1)} %collective-permute-done.1, bf16[1,3,16,3,1024]{4,3,2,1,0:T(4,128)(2,1)} %collective-permute-done, bf16[1,1,16,16,1024]{4,3,2,1,0:T(8,128)(2,1)S(1)} %copy-done.10, ...), kind=kLoop, calls=%fused_computation.67 | loop fusion | flops 7208960 | bytes 3604480 | tf_op jit(solution)/shard_map/squeeze | solution.py:146
  145.6 2.5 %subtract_bitcast_fusion = f32[1,1,16,16,1024]{4,3,2,1,0:T(8,128)} fusion(bf16[1,16,22,1024]{3,2,1,0:T(8,128)(2,1)S(1)} %get-tuple-element.34, bf16[1,16,16,1030]{3,2,1,0:T(8,128)(2,1)S(1)} %get-tuple-element.36), kind=kLoop, calls=%fused_computation.56 | loop fusion | flops 7602176 | bytes 7340032 | tf_op jit(solution)/shard_map/stack | solution.py:83
  148.1 2.1 %subtract_bitcast_fusion.2 = f32[1,1,16,16,1024]{4,3,2,1,0:T(8,128)} fusion(bf16[1,16,22,1024]{3,2,1,0:T(8,128)(2,1)S(1)} %get-tuple-element.33, bf16[1,1,16,1024]{3,2,1,0:T(8,128)(2,1)S(1)} %get-tuple-element.56, bf16[1,15,16,1024]{3,2,1,0:T(8,128)(2,1)S(1)} %get-tuple-element.58, bf16[1,15,16,1024]{3,2,1,0:T(8,128)(2,1)S(1)} %get-tuple-element.57, ...), kind=kLoop, calls=%fused_computation.58 | loop fusion | flops 9175040 | bytes 7340032 | tf_op jit(solution)/shard_map/stack | solution.py:83
  150.2 13.7 %fusion.9 = f32[1,3,16,16,1024]{4,3,2,1,0:T(8,128)} fusion(f32[1,3,16,16,1024]{4,3,2,1,0:T(8,128)S(1)} %copy-done, f32[1,3,16,16,3]{4,3,2,1,0:T(8,128)S(1)} %slice.592, f32[1,3,16,16,3]{4,3,2,1,0:T(8,128)} %slice.589, f32[1,3,16,22,1024]{4,3,2,1,0:T(8,128)S(1)} %bitcast.82, f32[1,1,16,16,1024]{4,3,2,1,0:T(8,128)} %subtract_bitcast_fusion, ...), kind=kLoop, calls=%fused_computation.17 | loop fusion | flops 44040192 | bytes 50354176 | tf_op jit(solution)/shard_map/sub | solution.py:88
  163.9 2.6 %fusion.28 = f32[1,3,16,16,1024]{4,3,2,1,0:T(8,128)} fusion(f32[1,3,16,16,1024]{4,3,2,1,0:T(8,128)} %fusion.9, f32[1,3,16,16,1024]{4,3,2,1,0:T(8,128)S(1)} %copy-done), kind=kLoop, calls=%fused_computation.49 | loop fusion | flops 524288 | bytes 3145728 | tf_op jit(solution)/shard_map/scatter-add | solution.py:89
  166.5 6.1 %multiply_add_fusion = (f32[1,3,16,16,1024]{4,3,2,1,0:T(8,128)}, f32[1,3,16,16,1024]{4,3,2,1,0:T(8,128)}) fusion(f32[1,3,16,16,1024]{4,3,2,1,0:T(8,128)S(1)} %copy-done, f32[1,3,16,16,1024]{4,3,2,1,0:T(8,128)} %fusion.28, f32[1,3,16,16,1024]{4,3,2,1,0:T(8,128)S(1)} %copy-done.11), kind=kLoop, calls=%fused_computation.42 | loop fusion | flops 3932160 | bytes 15728640 | tf_op jit(solution)/shard_map/add | solution.py:155
  (60 shorter events, 0.3 us)
Async XLA Ops:
  0.6 8.8 %copy-start = (f32[1,3,16,16,1024]{4,3,2,1,0:T(8,128)S(1)}, f32[1,3,16,16,1024]{4,3,2,1,0:T(8,128)}, u32[]{:S(2)}) copy-start(f32[1,3,16,16,1024]{4,3,2,1,0:T(8,128)} %param.6) | copy-start | bytes 9437188
  3.1 39.8 %all-to-all-start = ((bf16[16,3,1,16,1024]{4,3,2,1,0:T(8,128)(2,1)}), bf16[16,3,1,16,1024]{4,3,2,1,0:T(8,128)(2,1)}, u32[]{:S(2)}, u32[]{:S(2)}) async-start(bf16[16,3,1,16,1024]{4,3,2,1,0:T(8,128)(2,1)} %stack.24), calls=%async_computation | async-start | bytes 3145728 | tf_op jit(solution)/shard_map/all_to_all | solution.py:94
  11.6 9.8 %copy-start.6 = (bf16[1,3,16,16,1024]{4,3,2,1,0:T(8,128)(2,1)}, bf16[1,3,16,16,1024]{4,3,2,1,0:T(8,128)(2,1)S(1)}, u32[]{:S(2)}) copy-start(bf16[1,3,16,16,1024]{4,3,2,1,0:T(8,128)(2,1)S(1)} %get-tuple-element.31) | copy-start | bytes 4718596
  13.0 25.5 %collective-permute-start.2 = (bf16[1,3,16,3,1024]{4,3,2,1,0:T(4,128)(2,1)}, bf16[1,3,16,3,1024]{4,3,2,1,0:T(4,128)(2,1)}, u32[]{:S(2)}, u32[]{:S(2)}) collective-permute-start(bf16[1,3,16,3,1024]{4,3,2,1,0:T(4,128)(2,1)} %get-tuple-element.39), channel_id=1, source_target_pairs={{0,16},{16,32},{32,48},{48,64},{64,80},{80,96},{96,112},{112,128},... | collective-permute-start | bytes 884744 | tf_op jit(solution)/shard_map/ppermute | solution.py:22
  14.9 23.6 %collective-permute-start.3 = (bf16[1,3,16,3,1024]{4,3,2,1,0:T(4,128)(2,1)}, bf16[1,3,16,3,1024]{4,3,2,1,0:T(4,128)(2,1)}, u32[]{:S(2)}, u32[]{:S(2)}) collective-permute-start(bf16[1,3,16,3,1024]{4,3,2,1,0:T(4,128)(2,1)} %get-tuple-element.40), channel_id=1, source_target_pairs={{16,0},{32,16},{48,32},{64,48},{80,64},{96,80},{112,96},{128,112},... | collective-permute-start | bytes 884744 | tf_op jit(solution)/shard_map/ppermute | solution.py:23
  21.5 3.4 %copy-start.23 = (s32[2]{0:T(128)S(1)}, s32[2]{0:T(128)}, u32[]{:S(2)}) copy-start(s32[2]{0:T(128)} %param.9) | copy-start | bytes 28
  35.5 3.1 %copy-start.7 = (bf16[1,3,16,16,1024]{4,3,2,1,0:T(8,128)(2,1)S(1)}, bf16[1,3,16,16,1024]{4,3,2,1,0:T(8,128)(2,1)}, u32[]{:S(2)}) copy-start(bf16[1,3,16,16,1024]{4,3,2,1,0:T(8,128)(2,1)} %copy-done.6) | copy-start | bytes 4718596
  42.9 2.4 %copy-start.5 = (f32[1,3,16,16,1024]{4,3,2,1,0:T(8,128)S(1)}, f32[1,3,16,16,1024]{4,3,2,1,0:T(8,128)}, u32[]{:S(2)}) copy-start(f32[1,3,16,16,1024]{4,3,2,1,0:T(8,128)} %get-tuple-element.32) | copy-start | bytes 9437188
  46.2 8.7 %copy-start.1 = (bf16[1,16,16,1024]{3,2,1,0:T(8,128)(2,1)}, bf16[1,16,16,1024]{3,2,1,0:T(8,128)(2,1)S(1)}, u32[]{:S(2)}) copy-start(bf16[1,16,16,1024]{3,2,1,0:T(8,128)(2,1)S(1)} %get-tuple-element.16) | copy-start | bytes 1572868
  46.2 8.7 %copy-start.3 = (bf16[1,16,16,1024]{3,2,1,0:T(8,128)(2,1)}, bf16[1,16,16,1024]{3,2,1,0:T(8,128)(2,1)S(1)}, u32[]{:S(2)}) copy-start(bf16[1,16,16,1024]{3,2,1,0:T(8,128)(2,1)S(1)} %get-tuple-element.18) | copy-start | bytes 1572868
  46.2 8.7 %copy-start.9 = (bf16[1,1,16,16,1024]{4,3,2,1,0:T(8,128)(2,1)}, bf16[1,1,16,16,1024]{4,3,2,1,0:T(8,128)(2,1)S(1)}, u32[]{:S(2)}) copy-start(bf16[1,1,16,16,1024]{4,3,2,1,0:T(8,128)(2,1)S(1)} %get-tuple-element.17) | copy-start | bytes 1572868
  55.0 1.2 copy-start.8
  59.9 83.1 %collective-permute-start = (bf16[1,3,16,3,1024]{4,3,2,1,0:T(4,128)(2,1)}, bf16[1,3,16,3,1024]{4,3,2,1,0:T(4,128)(2,1)}, u32[]{:S(2)}, u32[]{:S(2)}) collective-permute-start(bf16[1,3,16,3,1024]{4,3,2,1,0:T(4,128)(2,1)} %get-tuple-element.37), channel_id=1, source_target_pairs={{0,16},{16,32},{32,48},{48,64},{64,80},{80,96},{96,112},{112,128},... | collective-permute-start | bytes 884744 | tf_op jit(solution)/shard_map/ppermute | solution.py:22
  60.0 83.0 %collective-permute-start.1 = (bf16[1,3,16,3,1024]{4,3,2,1,0:T(4,128)(2,1)}, bf16[1,3,16,3,1024]{4,3,2,1,0:T(4,128)(2,1)}, u32[]{:S(2)}, u32[]{:S(2)}) collective-permute-start(bf16[1,3,16,3,1024]{4,3,2,1,0:T(4,128)(2,1)} %get-tuple-element.38), channel_id=1, source_target_pairs={{16,0},{32,16},{48,32},{64,48},{80,64},{96,80},{112,96},{128,112},... | collective-permute-start | bytes 884744 | tf_op jit(solution)/shard_map/ppermute | solution.py:23
  139.0 3.0 %copy-start.4 = (bf16[1,16,16,1024]{3,2,1,0:T(8,128)(2,1)S(1)}, bf16[1,16,16,1024]{3,2,1,0:T(8,128)(2,1)}, u32[]{:S(2)}) copy-start(bf16[1,16,16,1024]{3,2,1,0:T(8,128)(2,1)} %copy-done.3) | copy-start | bytes 1572868
  139.0 3.1 %copy-start.12 = (f32[1,1,6,16,16,3]{5,4,3,2,1,0:T(8,128)S(1)}, f32[1,1,6,16,16,3]{5,4,3,2,1,0:T(8,128)}, u32[]{:S(2)}) copy-start(f32[1,1,6,16,16,3]{5,4,3,2,1,0:T(8,128)} %copy.23) | copy-start | bytes 55300
  139.0 3.1 %copy-start.13 = (f32[1,1,6,16,16,3]{5,4,3,2,1,0:T(8,128)S(1)}, f32[1,1,6,16,16,3]{5,4,3,2,1,0:T(8,128)}, u32[]{:S(2)}) copy-start(f32[1,1,6,16,16,3]{5,4,3,2,1,0:T(8,128)} %copy.24) | copy-start | bytes 55300
  142.0 1.1 copy-start.2
  142.0 1.3 copy-start.10
  143.4 6.8 %slice-start = ((s8[4718592]{0:T(1024)(128)(4,1)}), s8[4194304]{0:T(1024)(128)(4,1)S(1)}, s32[]{:S(2)}) async-start(s8[4718592]{0:T(1024)(128)(4,1)} %bitcast.81), calls=%async_computation.1 | async-start | bytes 8388608
  145.5 2.6 %copy-start.15 = (bf16[1,14,16,1024]{3,2,1,0:T(8,128)(2,1)S(1)}, bf16[1,14,16,1024]{3,2,1,0:T(8,128)(2,1)}, u32[]{:S(2)}) copy-start(bf16[1,14,16,1024]{3,2,1,0:T(8,128)(2,1)} %get-tuple-element.53) | copy-start | bytes 1376260
  145.5 2.6 %copy-start.16 = (bf16[1,14,16,1024]{3,2,1,0:T(8,128)(2,1)S(1)}, bf16[1,14,16,1024]{3,2,1,0:T(8,128)(2,1)}, u32[]{:S(2)}) copy-start(bf16[1,14,16,1024]{3,2,1,0:T(8,128)(2,1)} %get-tuple-element.54) | copy-start | bytes 1376260
  145.5 2.6 %copy-start.17 = (bf16[1,13,16,1024]{3,2,1,0:T(8,128)(2,1)S(1)}, bf16[1,13,16,1024]{3,2,1,0:T(8,128)(2,1)}, u32[]{:S(2)}) copy-start(bf16[1,13,16,1024]{3,2,1,0:T(8,128)(2,1)} %get-tuple-element.49) | copy-start | bytes 1277956
  145.5 2.6 %copy-start.18 = (bf16[1,13,16,1024]{3,2,1,0:T(8,128)(2,1)S(1)}, bf16[1,13,16,1024]{3,2,1,0:T(8,128)(2,1)}, u32[]{:S(2)}) copy-start(bf16[1,13,16,1024]{3,2,1,0:T(8,128)(2,1)} %get-tuple-element.50) | copy-start | bytes 1277956
  145.5 2.6 %copy-start.19 = (bf16[1,3,16,1024]{3,2,1,0:T(8,128)(2,1)S(1)}, bf16[1,3,16,1024]{3,2,1,0:T(8,128)(2,1)}, u32[]{:S(2)}) copy-start(bf16[1,3,16,1024]{3,2,1,0:T(8,128)(2,1)} %get-tuple-element.47) | copy-start | bytes 294916
  145.5 2.6 %copy-start.20 = (bf16[1,3,16,1024]{3,2,1,0:T(8,128)(2,1)S(1)}, bf16[1,3,16,1024]{3,2,1,0:T(8,128)(2,1)}, u32[]{:S(2)}) copy-start(bf16[1,3,16,1024]{3,2,1,0:T(8,128)(2,1)} %get-tuple-element.48) | copy-start | bytes 294916
  145.5 2.6 %copy-start.21 = (bf16[1,2,16,1024]{3,2,1,0:T(8,128)(2,1)S(1)}, bf16[1,2,16,1024]{3,2,1,0:T(8,128)(2,1)}, u32[]{:S(2)}) copy-start(bf16[1,2,16,1024]{3,2,1,0:T(8,128)(2,1)} %get-tuple-element.51) | copy-start | bytes 196612
  145.6 2.6 %copy-start.22 = (bf16[1,2,16,1024]{3,2,1,0:T(8,128)(2,1)S(1)}, bf16[1,2,16,1024]{3,2,1,0:T(8,128)(2,1)}, u32[]{:S(2)}) copy-start(bf16[1,2,16,1024]{3,2,1,0:T(8,128)(2,1)} %get-tuple-element.52) | copy-start | bytes 196612
  145.6 4.6 %slice-start.1 = ((s8[4718592]{0:T(1024)(128)(4,1)}), s8[524288]{0:T(1024)(128)(4,1)S(1)}, s32[]{:S(2)}) async-start(s8[4718592]{0:T(1024)(128)(4,1)} %bitcast.81), calls=%async_computation.2 | async-start | bytes 1048576
  148.1 2.1 %copy-start.14 = (f32[1,3,3,16,1024]{4,3,2,1,0:T(8,128)S(1)}, f32[1,3,3,16,1024]{4,3,2,1,0:T(8,128)}, u32[]{:S(2)}) copy-start(f32[1,3,3,16,1024]{4,3,2,1,0:T(8,128)} %get-tuple-element.19) | copy-start | bytes 1769476
  163.9 2.6 %copy-start.11 = (f32[1,3,16,16,1024]{4,3,2,1,0:T(8,128)S(1)}, f32[1,3,16,16,1024]{4,3,2,1,0:T(8,128)}, u32[]{:S(2)}) copy-start(f32[1,3,16,16,1024]{4,3,2,1,0:T(8,128)} %param.7) | copy-start | bytes 9437188
